TPU v7x, 512 devices: a whole 4x8x8 slice. The times are simulated.
512 devices in a mesh: img: 32 (over y, x_hi, core), patch: 16 (over z, x_lo).
Axes of the slice: x: 4 (x_hi: 2, x_lo: 2; x = x_hi * 2 + x_lo), y: 8, z: 8, core: 2. Of those that a mesh axis runs over, the one named last changes fastest.
Arguments:
- fresh: bfloat16 [32, 16, 4, 16, 4608], P('img', 'patch'), may hold values from -9 to 9
- stale_keys: bfloat16 [32, 16, 4, 16, 1536], P('img', 'patch'), may hold values from -6 to 6
- stale_values: bfloat16 [32, 16, 4, 16, 1536], P('img', 'patch'), may hold values from -6 to 6
- text_kv: bfloat16 [32, 128, 3072], P('img'), may hold values from -6 to 6
- group_slots: int32 [32], replicated, may hold values from 1 to 3, as said below
- text_len: int32 [32], replicated, may hold values from 1 to 128, as said below
Outputs:
- attended: bfloat16 [32, 16, 4, 16, 1536], P('img', 'patch')
Inputs may be any that keep to these rules, and one draw needn't show every extreme that they name: The groups hold 2 on average; the running sums over g of group_slots[g] - 2 differ by at most 1 between any two groups. `text_len`: some group has 128.
All inputs are finite; a program needn't handle non-finite values.
Results may differ from a plain program's by a relative error of at most 0.0046.
Values may be sent and summed in bfloat16 or wider, within the bound.
A program may use at most 64 MiB of HBM per device.

v0:
```python
import functools

import jax
import jax.numpy as jnp
from jax import lax
from jax.experimental import pallas as pl
from jax.experimental.pallas import tpu as pltpu
from jax.sharding import PartitionSpec as P

MESH = pl.DeviceIdType.MESH
F32 = jnp.float32
BF16 = jnp.bfloat16

HDIM = 128
HEADS = 12
HD = HDIM * HEADS
BLK = 16
LIVE = 3
TXT = 128
PEERS = 16
IMAGES = 32
ROWS = LIVE * BLK
BLOCKS = PEERS * LIVE
TBLOCKS = TXT // BLK
KEYS = BLOCKS * BLK + TXT
CHUNKS = 2
CPEERS = PEERS // CHUNKS
CROWS = CPEERS * ROWS
SCALE = 1.4426950408889634 / HDIM**0.5
MASKED = -1e30


def nt(a, b):
    return lax.dot_general(a, b, (((1,), (1,)), ((), ())), preferred_element_type=F32)


def owner_rank(peer, core):
    return ((peer >> 1) + 15 - 2 * core - (peer & 1)) & 3


def owned_head(peer, core):
    return (peer >> 3) * 6 + (peer & 1) * 3 + owner_rank(peer, core)


def partner(me, core, k):
    reach = k // 2 if k % 2 else -(k // 2)
    return (me + PEERS // 2 + reach * (1 - 2 * core)) & (PEERS - 1)


def kernel(
    fresh, keys, values, text, slots_in, lengths_in, out,
    own, stale, chunks, inbox, tkeys, tvalues, qmask, turned_keys, sbuf, pbuf, linv,
    osend, lsend, orecv, lrecv, ownout, ownlse, coef, counts,
    local_sem, text_sem, kq_sem, v_sem, o_sem, l_sem, kq_sent, v_sent, o_sent, l_sent, here,
):
    image = lax.axis_index("img")
    me = lax.axis_index("patch")
    core = image & 1
    is_owner = owner_rank(me, core) < 3
    my_head = owned_head(me, core)

    barrier = pltpu.get_barrier_semaphore()

    live = pl.ds(0, LIVE)
    local = [
        pltpu.make_async_copy(keys.at[live], stale.at[0], local_sem.at[0]),
        pltpu.make_async_copy(fresh.at[live], own, local_sem.at[1]),
        pltpu.make_async_copy(values.at[live], stale.at[1], local_sem.at[2]),
        pltpu.make_async_copy(slots_in, counts.at[0], local_sem.at[3]),
        pltpu.make_async_copy(lengths_in, counts.at[1], local_sem.at[4]),
    ]
    for copy in local:
        copy.start()

    def greet(peer, carry):
        pl.semaphore_signal(barrier, inc=1, device_id=(image, peer), device_id_type=MESH)
        return carry

    lax.fori_loop(me + 1, PEERS, greet, 0)

    @pl.when(me > 0)
    def _():
        pl.semaphore_wait(barrier, me)

    def tell(peer, carry):
        pl.semaphore_signal(here.at[me], inc=1, device_id=(image, peer), device_id_type=MESH)
        return carry

    lax.fori_loop(0, me, tell, 0)

    def text_copy(third, target):
        columns = pl.ds(pl.multiple_of(third * HD + my_head * HDIM, HDIM), HDIM)
        return pltpu.make_async_copy(text.at[:, :, columns], target, text_sem.at[third])

    texts = [text_copy(0, tkeys), text_copy(1, tvalues)]

    @pl.when(is_owner)
    def _():
        for copy in texts:
            copy.start()

    def stage(part, source):
        for head in range(HEADS):
            chunks[head, part] = source[:, :, head * HDIM : (head + 1) * HDIM]

    local[0].wait()
    stage(0, stale.at[0])
    local[1].wait()
    stage(1, own)
    local[2].wait()
    stage(2, stale.at[1])

    keys_queries = pl.ds(0, 2)
    only_values = pl.ds(2, 1)

    def send(peer, parts, sent, received):
        pltpu.make_async_remote_copy(
            src_ref=chunks.at[owned_head(peer, core), parts],
            dst_ref=inbox.at[me, parts],
            send_sem=sent,
            recv_sem=received,
            device_id=(image, peer),
            device_id_type=MESH,
        ).start()

    def send_before(parts, sent, received):
        for k in range(1, PEERS):
            peer = partner(me, core, k)

            @pl.when(jnp.logical_and(peer < me, owner_rank(peer, core) < 3))
            def _(peer=peer):
                send(peer, parts, sent, received)

    send_before(keys_queries, kq_sent, kq_sem)
    send_before(only_values, v_sent, v_sem)

    @pl.when(is_owner)
    def _():
        for parts, received in ((keys_queries, kq_sem), (only_values, v_sem)):
            pltpu.make_async_copy(chunks.at[my_head, parts], inbox.at[me, parts], received).start()

    def send_after(peer, carry):
        pl.semaphore_wait(here.at[peer], 1)

        @pl.when(owner_rank(peer, core) < 3)
        def _():
            send(peer, keys_queries, kq_sent, kq_sem)
            send(peer, only_values, v_sent, v_sem)

        return carry

    lax.fori_loop(me + 1, PEERS, send_after, 0)

    def wait_for(ref, sem):
        pltpu.make_async_copy(ref, ref, sem).wait()

    local[3].wait()
    local[4].wait()
    n = counts[0, image]
    length = counts[1, image]

    @pl.when(is_owner)
    def _():
        key = lax.broadcasted_iota(jnp.int32, (1, KEYS), 1)
        block = (key >> 4) + jnp.where(key < BLOCKS * BLK, 0, HDIM)
        slot = block - 3 * ((block * 171) >> 9)
        past = jnp.where(key < BLOCKS * BLK, slot - n, key - BLOCKS * BLK - length)
        mark = jnp.where(past >= 0, HDIM - 1, -1)
        row = lax.broadcasted_iota(jnp.int32, (HDIM, KEYS), 0)
        turned_keys[HDIM:] = jnp.where((row == block) | (row == mark), MASKED, 0.0).astype(BF16)
        shape = (BLOCKS, BLK, HDIM)
        block = lax.broadcasted_iota(jnp.int32, shape, 0)
        lane = lax.broadcasted_iota(jnp.int32, shape, 2)
        qmask[...] = jnp.where((lane == block) | (lane == HDIM - 1), 1.0, 0.0).astype(BF16)

    def attend_own(first, count):
        heads = range(first, first + count)
        diagonal = (
            lax.broadcasted_iota(jnp.int32, (ROWS, ROWS), 0) // BLK
            == lax.broadcasted_iota(jnp.int32, (ROWS, ROWS), 1) // BLK
        )

        def third(which, head):
            at = which * HD + head * HDIM
            return own[:, :, at : at + HDIM].reshape(ROWS, HDIM)

        scores = [jnp.where(diagonal, nt(third(0, head), third(1, head)), MASKED) for head in heads]
        tops = [jnp.max(x, axis=1, keepdims=True) for x in scores]
        weights = [jnp.exp2((x - top) * SCALE) for x, top in zip(scores, tops)]
        totals = [jnp.sum(x, axis=1, keepdims=True) for x in weights]
        sums = [
            jnp.dot(x.astype(BF16), third(2, head), preferred_element_type=F32) for x, head in zip(weights, heads)
        ]
        for i, head in enumerate(heads):
            ownout[head] = sums[i] / totals[i]
            ownlse[head] = jnp.broadcast_to(tops[i] * SCALE + jnp.log2(totals[i]), (ROWS, HDIM))

    def send_back(first, count, source, target, sent, received):
        for k in range(first, first + count):
            peer = partner(me, core, k)
            if k == PEERS:
                pltpu.make_async_copy(source.at[me], target, received).start()
            else:
                pltpu.make_async_remote_copy(
                    src_ref=source.at[peer],
                    dst_ref=target,
                    send_sem=sent,
                    recv_sem=received,
                    device_id=(image, peer),
                    device_id_type=MESH,
                ).start()

    @pl.when(is_owner)
    def _():
        for copy in texts:
            copy.wait()
        wait_for(inbox.at[:, keys_queries], kq_sem)
        k = jnp.concatenate([inbox[:, 0].reshape(BLOCKS * BLK, HDIM), tkeys[...].reshape(TXT, HDIM)], axis=0)
        turned_keys[:HDIM] = k.T
        q = jnp.concatenate(
            [inbox[:, 1].reshape(BLOCKS * BLK, HDIM), qmask[...].reshape(BLOCKS * BLK, HDIM)], axis=1
        )
        sbuf[...] = jnp.dot(q, turned_keys[...], preferred_element_type=F32)
        lane = lax.broadcasted_iota(jnp.int32, (ROWS, HDIM), 1)
        stats = jnp.zeros((ROWS, HDIM), F32)
        for peer in range(PEERS):
            rows = slice(peer * ROWS, (peer + 1) * ROWS)
            scores = sbuf[rows]
            top = jnp.max(scores, axis=1, keepdims=True)
            weights = jnp.exp2((scores - top) * SCALE)
            total = jnp.sum(weights, axis=1, keepdims=True)
            pbuf[peer] = weights.astype(BF16)
            linv[peer] = jnp.broadcast_to(1.0 / total, (ROWS, HDIM))
            stats = jnp.where(lane == peer, top * SCALE + jnp.log2(total), stats)
        turned = jnp.concatenate([stats, jnp.zeros((HDIM - ROWS, HDIM), F32)], axis=0).T
        for peer in range(PEERS):
            lsend[peer] = turned[peer : peer + 1]
        send_back(1, PEERS, lsend, lrecv.at[my_head], l_sent, l_sem)

        wait_for(inbox.at[:, only_values], v_sem)
        v = jnp.concatenate([inbox[:, 2].reshape(BLOCKS * BLK, HDIM), tvalues[...].reshape(TXT, HDIM)], axis=0)
        for chunk in range(CHUNKS):
            peers = [partner(me, core, chunk * CPEERS + i + 1) for i in range(CPEERS)]
            weights = jnp.concatenate([pbuf[peer] for peer in peers], axis=0)
            attended = jnp.dot(weights, v, preferred_element_type=F32)
            for i, peer in enumerate(peers):
                scaled = attended[i * ROWS : (i + 1) * ROWS] * linv[peer]
                osend[peer] = scaled.astype(BF16).reshape(LIVE, BLK, HDIM)
            send_back(chunk * CPEERS + 1, CPEERS, osend, orecv.at[my_head], o_sent, o_sem)

    attend_own(0, HEADS)

    @pl.when(is_owner)
    def _():
        wait_for(inbox.at[pl.ds(0, HEADS - 1), keys_queries], kq_sent)
        wait_for(inbox.at[pl.ds(0, HEADS - 1), only_values], v_sent)

    @pl.when(jnp.logical_not(is_owner))
    def _():
        wait_for(inbox.at[pl.ds(0, HEADS), keys_queries], kq_sent)
        wait_for(inbox.at[pl.ds(0, HEADS), only_values], v_sent)

    wait_for(lrecv, l_sem)
    stacked = jnp.concatenate([lrecv[head] for head in range(HEADS)] + [jnp.zeros((HDIM - HEADS, HDIM), F32)], axis=0)
    columns = stacked.T
    shown = lax.broadcasted_iota(jnp.int32, (LIVE, BLK, HDIM), 0) < n
    for head in range(HEADS):
        sibling = jnp.broadcast_to(columns[:ROWS, head : head + 1], (ROWS, HDIM))
        within = ownlse[head]
        top = jnp.maximum(sibling, within)
        a = jnp.exp2(sibling - top)
        b = jnp.exp2(within - top)
        inverse = 1.0 / (a + b)
        coef[head] = a * inverse
        ownout[head] = ownout[head] * (b * inverse)
    wait_for(orecv, o_sem)
    for head in range(HEADS):
        merged = orecv[head].reshape(ROWS, HDIM).astype(F32) * coef[head] + ownout[head]
        merged = jnp.where(shown, merged.reshape(LIVE, BLK, HDIM), 0.0)
        out[:, :, head * HDIM : (head + 1) * HDIM] = merged.astype(BF16)

    @pl.when(is_owner)
    def _():
        wait_for(lsend.at[pl.ds(0, PEERS - 1)], l_sent)
        wait_for(osend.at[pl.ds(0, PEERS - 1)], o_sent)


def attention(fresh, keys, values, text, slots, lengths):
    anywhere = pl.BlockSpec(memory_space=pl.ANY)
    semaphore = pltpu.SemaphoreType.DMA
    return pl.pallas_call(
        kernel,
        out_shape=jax.ShapeDtypeStruct((LIVE, BLK, HD), BF16),
        in_specs=[anywhere] * 6,
        out_specs=pl.BlockSpec(memory_space=pltpu.VMEM),
        scratch_shapes=[
            pltpu.VMEM((LIVE, BLK, 3 * HD), BF16),
            pltpu.VMEM((2, LIVE, BLK, HD), BF16),
            pltpu.VMEM((HEADS, 3, LIVE, BLK, HDIM), BF16),
            pltpu.VMEM((PEERS, 3, LIVE, BLK, HDIM), BF16),
            pltpu.VMEM((TBLOCKS, BLK, HDIM), BF16),
            pltpu.VMEM((TBLOCKS, BLK, HDIM), BF16),
            pltpu.VMEM((BLOCKS, BLK, HDIM), BF16),
            pltpu.VMEM((2 * HDIM, KEYS), BF16),
            pltpu.VMEM((BLOCKS * BLK, KEYS), F32),
            pltpu.VMEM((PEERS, ROWS, KEYS), BF16),
            pltpu.VMEM((PEERS, ROWS, HDIM), F32),
            pltpu.VMEM((PEERS, LIVE, BLK, HDIM), BF16),
            pltpu.VMEM((PEERS, 1, HDIM), F32),
            pltpu.VMEM((HEADS, LIVE, BLK, HDIM), BF16),
            pltpu.VMEM((HEADS, 1, HDIM), F32),
            pltpu.VMEM((HEADS, ROWS, HDIM), F32),
            pltpu.VMEM((HEADS, ROWS, HDIM), F32),
            pltpu.VMEM((HEADS, ROWS, HDIM), F32),
            pltpu.SMEM((2, IMAGES), jnp.int32),
            semaphore((5,)),
            semaphore((2,)),
        ]
        + [semaphore] * 8
        + [pltpu.SemaphoreType.REGULAR((PEERS,))],
        compiler_params=pltpu.CompilerParams(
            collective_id=0, has_side_effects=True, vmem_limit_bytes=24 * 1024 * 1024
        ),
    )(*[pltpu.with_memory_space_constraint(x, pltpu.HBM) for x in (fresh, keys, values, text, slots, lengths)])


def body(fresh, stale_keys, stale_values, text_kv, group_slots, text_len):
    slot_count = fresh.shape[2]
    text = text_kv[0].reshape(TBLOCKS, BLK, 2 * HD)
    merged = attention(fresh[0, 0], stale_keys[0, 0], stale_values[0, 0], text, group_slots, text_len)
    return jnp.pad(merged, ((0, slot_count - LIVE), (0, 0), (0, 0)))[None, None]


def solution(mesh):
    placed = (
        P("img", "patch", None, None, None),
        P("img", "patch", None, None, None),
        P("img", "patch", None, None, None),
        P("img", None, None),
        P(),
        P(),
    )
    return jax.shard_map(
        body,
        mesh=mesh,
        in_specs=placed,
        out_specs=P("img", "patch", None, None, None),
        check_vma=False,
    )
```

profile of v0, /device:TPU:56, one launch (start us, length us, event | category | flops | bytes accessed | tf_op | source)
XLA Modules:
  0.0 30.7 jit_solution(16209239581201867990)
XLA Ops:
  0.0 30.0 %shard_map.64 = bf16[3,16,1536]{2,1,0:T(8,128)(2,1)S(1)} custom-call(bf16[4,16,4608]{2,1,0:T(8,128)(2,1)} %bitcast.7, bf16[4,16,1536]{2,1,0:T(8,128)(2,1)} %bitcast.8, bf16[4,16,1536]{2,1,0:T(8,128)(2,1)} %bitcast.9, bf16[8,16,3072]{2,1,0:T(8,128)(2,1)} %bitcast.6, s32[32]{0:T(128)} %slots_in.1, s32[32]{0:T(128)} %lengths_in.1), custom_call_target="tpu_custom_call" | custom-call | tf_op jit(solution)/shard_map/pallas_call | solution.py:291
  30.0 0.7 %pad_bitcast_fusion = bf16[1,1,4,16,1536]{4,3,2,1,0:T(8,128)(2,1)} fusion(bf16[3,16,1536]{2,1,0:T(8,128)(2,1)S(1)} %shard_map.64), kind=kLoop, calls=%fused_computation | loop fusion | bytes 344064 | tf_op jit(solution)/shard_map/broadcast_in_dim | solution.py:331
where the time goes:
time: 30.9 us; the launch traced here: 30.7 us
  Pallas kernels  30 us (97%)
  local copies, waits for them, and re-layouts  0.69 us (2%)
    pallas_call x1, Pallas kernels, attention(): pl.pallas_call(kernel, out_shape=jax.ShapeDtypeStruct((LIVE, BLK, HD), BF...  30 us
    broadcast_in_dim x1, local copies, waits for them, and re-layouts, body(): return jnp.pad(merged, ((0, slot_count - LIVE), (0, 0), (0, 0)))[None, None]  0.69 us

commit v1 on v0

--- a/solution.py
+++ b/solution.py
@@ -49,9 +49,9 @@
 
 def kernel(
     fresh, keys, values, text, slots_in, lengths_in, out,
-    own, stale, chunks, inbox, tkeys, tvalues, qmask, turned_keys, sbuf, pbuf, linv,
+    own, inbox, tkeys, tvalues, qmask, turned_keys, sbuf, pbuf, linv,
     osend, lsend, orecv, lrecv, ownout, ownlse, coef, counts,
-    local_sem, text_sem, kq_sem, v_sem, o_sem, l_sem, kq_sent, v_sent, o_sent, l_sent, here,
+    local_sem, text_sem, part_sem, sent_sem, o_sem, l_sem, o_sent, l_sent, here,
 ):
     image = lax.axis_index("img")
     me = lax.axis_index("patch")
@@ -63,15 +63,10 @@
 
     live = pl.ds(0, LIVE)
     local = [
-        pltpu.make_async_copy(keys.at[live], stale.at[0], local_sem.at[0]),
-        pltpu.make_async_copy(fresh.at[live], own, local_sem.at[1]),
-        pltpu.make_async_copy(values.at[live], stale.at[1], local_sem.at[2]),
-        pltpu.make_async_copy(slots_in, counts.at[0], local_sem.at[3]),
-        pltpu.make_async_copy(lengths_in, counts.at[1], local_sem.at[4]),
+        pltpu.make_async_copy(fresh.at[live], own, local_sem.at[0]),
+        pltpu.make_async_copy(slots_in, counts.at[0], local_sem.at[1]),
+        pltpu.make_async_copy(lengths_in, counts.at[1], local_sem.at[2]),
     ]
-    for copy in local:
-        copy.start()
-
     def greet(peer, carry):
         pl.semaphore_signal(barrier, inc=1, device_id=(image, peer), device_id_type=MESH)
         return carry
@@ -94,58 +89,45 @@
 
     texts = [text_copy(0, tkeys), text_copy(1, tvalues)]
 
-    @pl.when(is_owner)
-    def _():
-        for copy in texts:
-            copy.start()
-
-    def stage(part, source):
-        for head in range(HEADS):
-            chunks[head, part] = source[:, :, head * HDIM : (head + 1) * HDIM]
-
-    local[0].wait()
-    stage(0, stale.at[0])
-    local[1].wait()
-    stage(1, own)
-    local[2].wait()
-    stage(2, stale.at[1])
-
-    keys_queries = pl.ds(0, 2)
-    only_values = pl.ds(2, 1)
-
-    def send(peer, parts, sent, received):
+    def piece(part, head):
+        columns = pl.ds(pl.multiple_of(head * HDIM, HDIM), HDIM)
+        return (keys, fresh, values)[part].at[live, :, columns]
+
+    def send(peer, part):
         pltpu.make_async_remote_copy(
-            src_ref=chunks.at[owned_head(peer, core), parts],
-            dst_ref=inbox.at[me, parts],
-            send_sem=sent,
-            recv_sem=received,
+            src_ref=piece(part, owned_head(peer, core)),
+            dst_ref=inbox.at[me, part],
+            send_sem=sent_sem.at[part],
+            recv_sem=part_sem.at[part],
             device_id=(image, peer),
             device_id_type=MESH,
         ).start()
 
-    def send_before(parts, sent, received):
+    for part in range(3):
         for k in range(1, PEERS):
             peer = partner(me, core, k)
 
             @pl.when(jnp.logical_and(peer < me, owner_rank(peer, core) < 3))
-            def _(peer=peer):
-                send(peer, parts, sent, received)
-
-    send_before(keys_queries, kq_sent, kq_sem)
-    send_before(only_values, v_sent, v_sem)
-
-    @pl.when(is_owner)
-    def _():
-        for parts, received in ((keys_queries, kq_sem), (only_values, v_sem)):
-            pltpu.make_async_copy(chunks.at[my_head, parts], inbox.at[me, parts], received).start()
+            def _(peer=peer, part=part):
+                send(peer, part)
+
+    @pl.when(is_owner)
+    def _():
+        for part in range(3):
+            pltpu.make_async_copy(piece(part, my_head), inbox.at[me, part], part_sem.at[part]).start()
+        for copy in texts:
+            copy.start()
+
+    for copy in local:
+        copy.start()
 
     def send_after(peer, carry):
         pl.semaphore_wait(here.at[peer], 1)
 
         @pl.when(owner_rank(peer, core) < 3)
         def _():
-            send(peer, keys_queries, kq_sent, kq_sem)
-            send(peer, only_values, v_sent, v_sem)
+            for part in range(3):
+                send(peer, part)
 
         return carry
 
@@ -154,8 +136,8 @@
     def wait_for(ref, sem):
         pltpu.make_async_copy(ref, ref, sem).wait()
 
-    local[3].wait()
-    local[4].wait()
+    for copy in local:
+        copy.wait()
     n = counts[0, image]
     length = counts[1, image]
 
@@ -214,9 +196,10 @@
     def _():
         for copy in texts:
             copy.wait()
-        wait_for(inbox.at[:, keys_queries], kq_sem)
+        wait_for(inbox.at[:, 0], part_sem.at[0])
         k = jnp.concatenate([inbox[:, 0].reshape(BLOCKS * BLK, HDIM), tkeys[...].reshape(TXT, HDIM)], axis=0)
         turned_keys[:HDIM] = k.T
+        wait_for(inbox.at[:, 1], part_sem.at[1])
         q = jnp.concatenate(
             [inbox[:, 1].reshape(BLOCKS * BLK, HDIM), qmask[...].reshape(BLOCKS * BLK, HDIM)], axis=1
         )
@@ -237,7 +220,7 @@
             lsend[peer] = turned[peer : peer + 1]
         send_back(1, PEERS, lsend, lrecv.at[my_head], l_sent, l_sem)
 
-        wait_for(inbox.at[:, only_values], v_sem)
+        wait_for(inbox.at[:, 2], part_sem.at[2])
         v = jnp.concatenate([inbox[:, 2].reshape(BLOCKS * BLK, HDIM), tvalues[...].reshape(TXT, HDIM)], axis=0)
         for chunk in range(CHUNKS):
             peers = [partner(me, core, chunk * CPEERS + i + 1) for i in range(CPEERS)]
@@ -252,13 +235,13 @@
 
     @pl.when(is_owner)
     def _():
-        wait_for(inbox.at[pl.ds(0, HEADS - 1), keys_queries], kq_sent)
-        wait_for(inbox.at[pl.ds(0, HEADS - 1), only_values], v_sent)
+        for part in range(3):
+            wait_for(inbox.at[pl.ds(0, HEADS - 1), part], sent_sem.at[part])
 
     @pl.when(jnp.logical_not(is_owner))
     def _():
-        wait_for(inbox.at[pl.ds(0, HEADS), keys_queries], kq_sent)
-        wait_for(inbox.at[pl.ds(0, HEADS), only_values], v_sent)
+        for part in range(3):
+            wait_for(inbox.at[pl.ds(0, HEADS), part], sent_sem.at[part])
 
     wait_for(lrecv, l_sem)
     stacked = jnp.concatenate([lrecv[head] for head in range(HEADS)] + [jnp.zeros((HDIM - HEADS, HDIM), F32)], axis=0)
@@ -295,8 +278,6 @@
         out_specs=pl.BlockSpec(memory_space=pltpu.VMEM),
         scratch_shapes=[
             pltpu.VMEM((LIVE, BLK, 3 * HD), BF16),
-            pltpu.VMEM((2, LIVE, BLK, HD), BF16),
-            pltpu.VMEM((HEADS, 3, LIVE, BLK, HDIM), BF16),
             pltpu.VMEM((PEERS, 3, LIVE, BLK, HDIM), BF16),
             pltpu.VMEM((TBLOCKS, BLK, HDIM), BF16),
             pltpu.VMEM((TBLOCKS, BLK, HDIM), BF16),
@@ -313,10 +294,12 @@
             pltpu.VMEM((HEADS, ROWS, HDIM), F32),
             pltpu.VMEM((HEADS, ROWS, HDIM), F32),
             pltpu.SMEM((2, IMAGES), jnp.int32),
-            semaphore((5,)),
+            semaphore((3,)),
             semaphore((2,)),
+            semaphore((3,)),
+            semaphore((3,)),
         ]
-        + [semaphore] * 8
+        + [semaphore] * 4
         + [pltpu.SemaphoreType.REGULAR((PEERS,))],
         compiler_params=pltpu.CompilerParams(
             collective_id=0, has_side_effects=True, vmem_limit_bytes=24 * 1024 * 1024

time: 30.9 us -> 30.9 us (level)
  no operation moved by 1% of the time
where the time goes in v1:
time: 30.9 us; the launch traced here: 30.8 us
  Pallas kernels  30.1 us (97%)
  local copies, waits for them, and re-layouts  0.69 us (2%)
    pallas_call x1, Pallas kernels, attention(): pl.pallas_call(kernel, out_shape=jax.ShapeDtypeStruct((LIVE, BLK, HD), BF...  30.1 us
    broadcast_in_dim x1, local copies, waits for them, and re-layouts, body(): return jnp.pad(merged, ((0, slot_count - LIVE), (0, 0), (0, 0)))[None, None]  0.69 us

profile of v1, /device:TPU:56, one launch (start us, length us, event | category | flops | bytes accessed | tf_op | source)
XLA Modules:
  0.0 30.8 jit_solution(16327977850138936152)
XLA Ops:
  0.0 30.1 %shard_map.64 = bf16[3,16,1536]{2,1,0:T(8,128)(2,1)S(1)} custom-call(bf16[4,16,4608]{2,1,0:T(8,128)(2,1)} %bitcast.7, bf16[4,16,1536]{2,1,0:T(8,128)(2,1)} %bitcast.8, bf16[4,16,1536]{2,1,0:T(8,128)(2,1)} %bitcast.9, bf16[8,16,3072]{2,1,0:T(8,128)(2,1)} %bitcast.6, s32[32]{0:T(128)} %slots_in.1, s32[32]{0:T(128)} %lengths_in.1), custom_call_target="tpu_custom_call" | custom-call | tf_op jit(solution)/shard_map/pallas_call | solution.py:274
  30.1 0.7 %pad_bitcast_fusion = bf16[1,1,4,16,1536]{4,3,2,1,0:T(8,128)(2,1)} fusion(bf16[3,16,1536]{2,1,0:T(8,128)(2,1)S(1)} %shard_map.64), kind=kLoop, calls=%fused_computation | loop fusion | bytes 344064 | tf_op jit(solution)/shard_map/broadcast_in_dim | solution.py:314

commit v2 on v0

--- a/solution.py
+++ b/solution.py
@@ -131,7 +131,34 @@
             def _(peer=peer):
                 send(peer, parts, sent, received)
 
+    def attend_own(first, count):
+        heads = range(first, first + count)
+        diagonal = (
+            lax.broadcasted_iota(jnp.int32, (ROWS, ROWS), 0) // BLK
+            == lax.broadcasted_iota(jnp.int32, (ROWS, ROWS), 1) // BLK
+        )
+
+        def third(which, head):
+            at = which * HD + head * HDIM
+            return own[:, :, at : at + HDIM].reshape(ROWS, HDIM)
+
+        scores = [jnp.where(diagonal, nt(third(0, head), third(1, head)), MASKED) for head in heads]
+        tops = [jnp.max(x, axis=1, keepdims=True) for x in scores]
+        weights = [jnp.exp2((x - top) * SCALE) for x, top in zip(scores, tops)]
+        totals = [jnp.sum(x, axis=1, keepdims=True) for x in weights]
+        sums = [
+            jnp.dot(x.astype(BF16), third(2, head), preferred_element_type=F32) for x, head in zip(weights, heads)
+        ]
+        for i, head in enumerate(heads):
+            ownout[head] = sums[i] / totals[i]
+            ownlse[head] = jnp.broadcast_to(tops[i] * SCALE + jnp.log2(totals[i]), (ROWS, HDIM))
+
     send_before(keys_queries, kq_sent, kq_sem)
+
+    @pl.when(core == 1)
+    def _():
+        attend_own(0, HEADS)
+
     send_before(only_values, v_sent, v_sem)
 
     @pl.when(is_owner)
@@ -172,28 +199,6 @@
         block = lax.broadcasted_iota(jnp.int32, shape, 0)
         lane = lax.broadcasted_iota(jnp.int32, shape, 2)
         qmask[...] = jnp.where((lane == block) | (lane == HDIM - 1), 1.0, 0.0).astype(BF16)
-
-    def attend_own(first, count):
-        heads = range(first, first + count)
-        diagonal = (
-            lax.broadcasted_iota(jnp.int32, (ROWS, ROWS), 0) // BLK
-            == lax.broadcasted_iota(jnp.int32, (ROWS, ROWS), 1) // BLK
-        )
-
-        def third(which, head):
-            at = which * HD + head * HDIM
-            return own[:, :, at : at + HDIM].reshape(ROWS, HDIM)
-
-        scores = [jnp.where(diagonal, nt(third(0, head), third(1, head)), MASKED) for head in heads]
-        tops = [jnp.max(x, axis=1, keepdims=True) for x in scores]
-        weights = [jnp.exp2((x - top) * SCALE) for x, top in zip(scores, tops)]
-        totals = [jnp.sum(x, axis=1, keepdims=True) for x in weights]
-        sums = [
-            jnp.dot(x.astype(BF16), third(2, head), preferred_element_type=F32) for x, head in zip(weights, heads)
-        ]
-        for i, head in enumerate(heads):
-            ownout[head] = sums[i] / totals[i]
-            ownlse[head] = jnp.broadcast_to(tops[i] * SCALE + jnp.log2(totals[i]), (ROWS, HDIM))
 
     def send_back(first, count, source, target, sent, received):
         for k in range(first, first + count):
@@ -248,7 +253,9 @@
                 osend[peer] = scaled.astype(BF16).reshape(LIVE, BLK, HDIM)
             send_back(chunk * CPEERS + 1, CPEERS, osend, orecv.at[my_head], o_sent, o_sem)
 
-    attend_own(0, HEADS)
+    @pl.when(core == 0)
+    def _():
+        attend_own(0, HEADS)
 
     @pl.when(is_owner)
     def _():

time: 30.9 us -> 30.9 us (level)
  no operation moved by 1% of the time
where the time goes in v2:
time: 30.9 us; the launch traced here: 30.7 us
  Pallas kernels  30 us (97%)
  local copies, waits for them, and re-layouts  0.69 us (2%)
    pallas_call x1, Pallas kernels, attention(): pl.pallas_call(kernel, out_shape=jax.ShapeDtypeStruct((LIVE, BLK, HD), BF...  30 us
    broadcast_in_dim x1, local copies, waits for them, and re-layouts, body(): return jnp.pad(merged, ((0, slot_count - LIVE), (0, 0), (0, 0)))[None, None]  0.69 us

profile of v2, /device:TPU:56, one launch (start us, length us, event | category | flops | bytes accessed | tf_op | source)
XLA Modules:
  0.0 30.7 jit_solution(16069457944810452040)
XLA Ops:
  0.0 30.0 %shard_map.64 = bf16[3,16,1536]{2,1,0:T(8,128)(2,1)S(1)} custom-call(bf16[4,16,4608]{2,1,0:T(8,128)(2,1)} %bitcast.7, bf16[4,16,1536]{2,1,0:T(8,128)(2,1)} %bitcast.8, bf16[4,16,1536]{2,1,0:T(8,128)(2,1)} %bitcast.9, bf16[8,16,3072]{2,1,0:T(8,128)(2,1)} %bitcast.6, s32[32]{0:T(128)} %slots_in.1, s32[32]{0:T(128)} %lengths_in.1), custom_call_target="tpu_custom_call" | custom-call | tf_op jit(solution)/shard_map/pallas_call | solution.py:298
  30.0 0.7 %pad_bitcast_fusion = bf16[1,1,4,16,1536]{4,3,2,1,0:T(8,128)(2,1)} fusion(bf16[3,16,1536]{2,1,0:T(8,128)(2,1)S(1)} %shard_map.64), kind=kLoop, calls=%fused_computation | loop fusion | bytes 344064 | tf_op jit(solution)/shard_map/broadcast_in_dim | solution.py:338
